TPU v7x, 32 devices: a whole 2x2x4 slice. The times are simulated.
32 devices in a mesh: dp: 4 (over y, x), mp: 8 (over z, core).
Axes of the slice: x: 2, y: 2, z: 4, core: 2. Of those that a mesh axis runs over, the one named last changes fastest.
Arguments:
- tokens: bfloat16 [2048, 8192], P(('dp', 'mp')), may hold values from -6 to 6
- row_counts: int32 [4, 8], replicated, may hold values from 8 to 64, as said below
- gate_blocks: bfloat16 [64, 16, 128, 256], P('mp'), may hold values from -0.125 to 0.125
- gate_index: int32 [64, 16], P('mp'), may hold values from 0 to 63, as said below
- up_blocks: bfloat16 [64, 16, 128, 256], P('mp'), may hold values from -0.125 to 0.125
- up_index: int32 [64, 16], P('mp'), may hold values from 0 to 63, as said below
- down_blocks: bfloat16 [64, 16, 256, 128], P('mp'), may hold values from -0.09375 to 0.09375
- down_index: int32 [64, 16], P('mp'), may hold values from 0 to 63, as said below
Outputs:
- layer_out: bfloat16 [2048, 8192], P(('dp', 'mp'))
Inputs may be any that keep to these rules, and one draw needn't show every extreme that they name: `row_counts`: every entry is a multiple of 8; the entries of one column (one mp index) add up to 32 times the number of dp indices, and every column holds one entry equal to 64. `gate_index`: each row holds 16 distinct block rows in increasing order. `up_index`: each row holds 16 distinct block rows in increasing order. `down_index`: each row holds 16 distinct block columns in increasing order.
All inputs are finite; a program needn't handle non-finite values.
Results may differ from a plain program's by a relative error of at most 0.013.
Values may be sent and summed in bfloat16 or wider, within the bound.
A program may use at most 192 MiB of HBM per device.

v0:
```python
import jax
import jax.numpy as jnp
from jax import lax
from jax.sharding import PartitionSpec as P


def make_hidden(row_block, gate_blocks, gate_index, up_blocks, up_index):
    row_count = row_block.shape[0]
    block_width = gate_blocks.shape[2]
    split_rows = row_block.reshape(row_count, -1, block_width)
    gate_input = jnp.take(split_rows, gate_index, axis=1)
    up_input = jnp.take(split_rows, up_index, axis=1)
    gate_value = jnp.einsum(
        "rjkc,jkcn->rjn", gate_input, gate_blocks, preferred_element_type=jnp.float32
    )
    up_value = jnp.einsum("rjkc,jkcn->rjn", up_input, up_blocks, preferred_element_type=jnp.float32)
    hidden = (jax.nn.silu(gate_value) * up_value).astype(jnp.bfloat16)
    return hidden.reshape(row_count, -1)


def apply_down(hidden_rows, down_blocks, down_index, block_total):
    row_count = hidden_rows.shape[0]
    column_blocks = down_blocks.shape[0]
    nonzero_count = down_blocks.shape[1]
    block_width = down_blocks.shape[3]
    hidden_split = hidden_rows.reshape(row_count, column_blocks, down_blocks.shape[2])
    products = jnp.einsum(
        "rjn,jknc->rjkc", hidden_split, down_blocks, preferred_element_type=jnp.float32
    )
    flat_products = products.reshape(row_count, column_blocks * nonzero_count, block_width)
    placed = jnp.zeros((row_count, block_total, block_width), jnp.float32)
    placed = placed.at[:, down_index.reshape(-1)].add(flat_products)
    return placed.reshape(row_count, -1)


def body(tokens, row_counts, gate_blocks, gate_index, up_blocks, up_index, down_blocks, down_index):
    dp_size = lax.axis_size("dp")
    own_mp = lax.axis_index("mp")
    rows_in = tokens.shape[0]
    model_width = tokens.shape[1]
    block_total = model_width // down_blocks.shape[3]
    lane_counts = lax.dynamic_slice_in_dim(row_counts, own_mp, 1, 1)[:, 0]
    per_source = lane_counts // dp_size
    run_ends = jnp.cumsum(per_source)
    starts = run_ends - per_source
    balanced = rows_in // 2
    position = jnp.arange(balanced, dtype=jnp.int32)
    source = jnp.sum((position[:, None] >= run_ends[None, :]).astype(jnp.int32), axis=1)
    offset = position - jnp.take(starts, source)
    flat_index = offset * dp_size + source
    slot_rows = rows_in // dp_size
    received = lax.all_to_all(
        tokens.reshape(slot_rows, dp_size, model_width),
        "dp",
        split_axis=1,
        concat_axis=1,
        tiled=True,
    )
    chosen_rows = jnp.take(received.reshape(slot_rows * dp_size, model_width), flat_index, axis=0)
    hidden_all = make_hidden(
        lax.all_gather(chosen_rows, "mp", axis=0, tiled=True),
        gate_blocks,
        gate_index,
        up_blocks,
        up_index,
    )
    summed = lax.psum_scatter(
        apply_down(hidden_all, down_blocks, down_index, block_total).astype(jnp.bfloat16),
        "mp",
        scatter_dimension=0,
        tiled=True,
    )
    returned = (
        jnp.zeros((slot_rows * dp_size, model_width), jnp.bfloat16).at[flat_index].set(summed)
    )
    back_rows = lax.all_to_all(
        returned.reshape(slot_rows, dp_size, model_width),
        "dp",
        split_axis=1,
        concat_axis=1,
        tiled=True,
    )
    return back_rows.reshape(rows_in, model_width)


def solution(mesh):
    in_specs = (
        P(("dp", "mp"), None),
        P(),
        P("mp", None, None, None),
        P("mp", None),
        P("mp", None, None, None),
        P("mp", None),
        P("mp", None, None, None),
        P("mp", None),
    )
    out_specs = P(("dp", "mp"), None)
    return jax.shard_map(body, mesh=mesh, in_specs=in_specs, out_specs=out_specs, check_vma=False)
```

profile of v0, /device:TPU:0, one launch (start us, length us, event | category | flops | bytes accessed | tf_op | source)
XLA Modules:
  0.0 261.8 jit_solution(5761530390924047115)
XLA Ops:
  6.5 1.5 reshape.143
  8.0 1.5 copy.31
  9.6 5.2 %all-to-all-start = ((bf16[16,4,8192]{2,0,1:T(8,128)(2,1)}), bf16[16,4,8192]{2,0,1:T(8,128)(2,1)S(1)}, u32[]{:S(2)}, u32[]{:S(2)}) async-start(bf16[16,4,8192]{2,0,1:T(8,128)(2,1)} %copy.31), calls=%async_computation | async-start | bytes 2097152 | tf_op jit(solution)/shard_map/all_to_all | solution.py:52
  14.8 0.9 dynamic-slice_reduce_fusion
  15.7 0.1 reduce
  15.8 0.7 fusion.36
  16.6 2.5 fusion.29
  19.1 2.5 compare_and_fusion.2
  21.6 6.8 %all-to-all-done = bf16[16,4,8192]{2,0,1:T(8,128)(2,1)S(1)} async-done(((bf16[16,4,8192]{2,0,1:T(8,128)(2,1)}), bf16[16,4,8192]{2,0,1:T(8,128)(2,1)S(1)}, u32[]{:S(2)}, u32[]{:S(2)}) %all-to-all-start) | async-done | bytes 1048608 | tf_op jit(solution)/shard_map/all_to_all | solution.py:52
  28.4 0.8 copy.32
  29.2 0.3 reshape.144
  29.5 0.9 gather_fusion
  30.4 0.9 broadcast_select_fusion
  31.3 0.2 reduce-scatter.4.cloned.1.call-start
  31.9 47.1 %all-gather.2.cloned.1.call-done = bf16[256,8192]{1,0:T(8,128)(2,1)} async-done(((bf16[32,8192]{1,0:T(8,128)(2,1)}), bf16[256,8192]{1,0:T(8,128)(2,1)}) %all-gather.2.cloned.1.call-update) | async-done | bytes 4194320 | tf_op jit(solution)/shard_map/all_gather | solution.py:61
  78.9 5.4 %copy_bitcast_fusion = bf16[256,64,128]{2,0,1:T(8,128)(2,1)} fusion(bf16[256,8192]{1,0:T(8,128)(2,1)} %all-gather.2.cloned.1.call-done), kind=kLoop, calls=%fused_computation.13 | loop fusion | bytes 8388608 | tf_op jit(solution)/shard_map/reshape | solution.py:10
  84.3 8.7 %gather_fusion.2 = bf16[128,256,128]{2,1,0:T(8,128)(2,1)} fusion(bf16[256,64,128]{2,0,1:T(8,128)(2,1)} %copy_bitcast_fusion, s32[1024]{0:T(1024)S(1)} %pad_clamp_fusion), kind=kCustom, calls=%fused_computation.1.clone | custom fusion | bytes 16777728 | tf_op jit(solution)/shard_map/jit(_take)/gather | solution.py:12
  93.0 8.7 %gather_fusion.1 = bf16[128,256,128]{2,1,0:T(8,128)(2,1)} fusion(bf16[256,64,128]{2,0,1:T(8,128)(2,1)} %copy_bitcast_fusion, s32[1024]{0:T(1024)S(1)} %pad_clamp_fusion.1), kind=kCustom, calls=%fused_computation.clone | custom fusion | bytes 16777728 | tf_op jit(solution)/shard_map/jit(_take)/gather | solution.py:11
  101.8 7.7 %fusion.2 = f32[8,256,256,1]{2,1,3,0:T(8,128)S(1)} fusion(bf16[8,16,128,256]{3,2,1,0:T(8,128)(2,1)} %param.12, bf16[8,16,256,128]{3,2,1,0:T(8,128)(2,1)} %bitcast.95, pred[8,16]{1,0:T(8,128)(4,1)S(1)} %compare_and_fusion.1), kind=kOutput, calls=%fused_computation.7 | convolution fusion | flops 2151677952 | bytes 18874496 | tf_op jit(solution)/shard_map/rjkc,jkcn->rjn/dot_general | solution.py:13
  109.5 14.1 %fusion.20 = f32[8,256,16,128]{3,1,2,0:T(8,128)} fusion(bf16[8,16,256,128]{3,2,1,0:T(8,128)(2,1)} %param.16, bf16[8,16,128,256]{3,2,1,0:T(8,128)(2,1)} %param.14, bf16[8,16,256,128]{3,2,1,0:T(8,128)(2,1)} %bitcast.94, pred[8,16]{1,0:T(8,128)(4,1)S(1)} %compare_and_fusion, f32[8,256,256,1]{2,1,3,0:T(8,128)S(1)} %fusion.2), kind=kOutput, calls=%fused_computation.24 | convolution fusion | flops 4302307328 | bytes 44040320 | tf_op jit(solution)/shard_map/rjn,jknc->rjkc/dot_general | solution.py:27
  123.6 4.2 %broadcast_in_dim.39 = f32[256,64,128]{2,0,1:T(8,128)} broadcast(f32[]{:T(128)} %constant.73.clone.1), dimensions={} | broadcast | bytes 8388612 | tf_op jit(solution)/shard_map/broadcast_in_dim | solution.py:31
  127.8 39.0 %scatter_fusion = f32[256,64,128]{2,0,1:T(8,128)} fusion(f32[256,64,128]{2,0,1:T(8,128)} %broadcast_in_dim.39, s32[128]{0:T(128)S(1)} %fusion.30, f32[128,256,128]{2,1,0:T(8,128)} %bitcast.92), kind=kCustom, calls=%fused_computation.3 | custom fusion | flops 4194304 | bytes 50332160 | tf_op jit(solution)/shard_map/scatter-add | solution.py:32
  166.8 6.0 %convert_element_type.14 = bf16[256,64,128]{2,0,1:T(8,128)(2,1)} convert(f32[256,64,128]{2,0,1:T(8,128)} %scatter_fusion) | non-fusion elementwise | flops 2097152 | bytes 12582912 | tf_op jit(solution)/shard_map/convert_element_type | solution.py:68
  172.9 6.4 %copy.35 = bf16[256,64,128]{0,2,1:T(8,128)(2,1)} copy(bf16[256,64,128]{2,0,1:T(8,128)(2,1)} %convert_element_type.14) | data formatting | bytes 8388608 | tf_op jit(solution)/shard_map/convert_element_type | solution.py:68
  179.3 6.4 %copy.42 = bf16[256,8192]{1,0:T(8,128)(2,1)} copy(bf16[256,8192]{0,1:T(8,128)(2,1)} %bitcast.93) | data formatting | bytes 8388608
  185.7 48.8 %reduce-scatter.4.cloned.1.call-done = bf16[32,8192]{1,0:T(8,128)(2,1)} async-done(((bf16[256,8192]{1,0:T(8,128)(2,1)}), bf16[32,8192]{1,0:T(8,128)(2,1)}) %reduce-scatter.4.cloned.1.call-update) | async-done | bytes 524304 | tf_op jit(solution)/shard_map/reduce_scatter | solution.py:67
  234.4 2.2 scatter_custom_fusion.1
  236.6 0.4 reshape.147
  237.0 0.6 copy.37
  237.6 15.4 %all_to_all.10 = bf16[16,4,8192]{2,0,1:T(8,128)(2,1)S(1)} all-to-all(bf16[16,4,8192]{2,0,1:T(8,128)(2,1)S(1)} %copy.37), channel_id=1, replica_groups=mesh['dp'=4,'mp'=8] {'dp'}, dimensions={1} | all-to-all | bytes 2097152 | tf_op jit(solution)/shard_map/all_to_all | solution.py:76
  253.1 0.8 copy.38
  253.9 1.1 reshape.148
  (23 shorter events, 0.5 us)
Async XLA Ops:
  6.5 25.0 %copy-start.2 = (s32[8,16]{1,0:T(8,128)S(1)}, s32[8,16]{1,0:T(8,128)}, u32[]{:S(2)}) copy-start(s32[8,16]{1,0:T(8,128)} %param.17) | copy-start | bytes 1540
  6.5 25.1 %copy-start = (s32[8,16]{1,0:T(8,128)S(1)}, s32[8,16]{1,0:T(8,128)}, u32[]{:S(2)}) copy-start(s32[8,16]{1,0:T(8,128)} %param.13) | copy-start | bytes 1540
  6.5 25.2 %copy-start.1 = (s32[8,16]{1,0:T(8,128)S(1)}, s32[8,16]{1,0:T(8,128)}, u32[]{:S(2)}) copy-start(s32[8,16]{1,0:T(8,128)} %param.15) | copy-start | bytes 1540
  9.6 18.8 %all-to-all-start = ((bf16[16,4,8192]{2,0,1:T(8,128)(2,1)}), bf16[16,4,8192]{2,0,1:T(8,128)(2,1)S(1)}, u32[]{:S(2)}, u32[]{:S(2)}) async-start(bf16[16,4,8192]{2,0,1:T(8,128)(2,1)} %copy.31), calls=%async_computation | async-start | bytes 2097152 | tf_op jit(solution)/shard_map/all_to_all | solution.py:52
  14.8 64.2 %all-gather.2.cloned.1.call-start = ((), (), s32[]{:S(2)}) async-start(), calls=%async_computation.3 | async-start | bytes 4718592 | tf_op jit(solution)/shard_map/all_gather | solution.py:61
  31.3 203.1 %reduce-scatter.4.cloned.1.call-start = ((), (), s32[]{:S(2)}) async-start(), calls=%async_computation.4 | async-start | bytes 4718592 | tf_op jit(solution)/shard_map/reduce_scatter | solution.py:67
Sparse Core Ops, SparseCore 0:
  31.4 47.4 all-gather.1
  185.8 48.6 reduce-scatter.3
where the time goes:
time: 263 us; the launch traced here: 262 us
  waiting for transfers between devices  103 us (39%)
  other arithmetic  52.2 us (20%)
  local copies, waits for them, and re-layouts  50.8 us (19%)
  matrix products  21.8 us (8%)
  blocking collectives  15.4 us (6%)
  between operations  13.5 us (5%)
  starting transfers between devices  5.39 us (2%)
    reduce_scatter x1, waiting for transfers between devices, body(): lax.psum_scatter(apply_down(hidden_all, down_blocks, down_index, block_to...  48.8 us
    all_gather x1, waiting for transfers between devices, body(): lax.all_gather(chosen_rows, 'mp', axis=0, tiled=True)  47.1 us
    scatter-add x1, other arithmetic, apply_down(): placed = placed.at[:, down_index.reshape(-1)].add(flat_products)  39 us
    all_to_all x1, blocking collectives, body(): lax.all_to_all(returned.reshape(slot_rows, dp_size, model_width), 'dp', s...  15.4 us
    dot_general x1, matrix products, apply_down(): jnp.einsum('rjn,jknc->rjkc', hidden_split, down_blocks, preferred_element...  14.1 us
    gather x1, local copies, waits for them, and re-layouts, make_hidden(): up_input = jnp.take(split_rows, up_index, axis=1)  8.74 us
    gather x1, local copies, waits for them, and re-layouts, make_hidden(): gate_input = jnp.take(split_rows, gate_index, axis=1)  8.74 us
    dot_general x1, matrix products, make_hidden(): jnp.einsum('rjkc,jkcn->rjn', gate_input, gate_blocks, preferred_element_t...  7.67 us
  transfers between devices with their start and end apart: 3, of which 3 were waited for; matrix products, arithmetic and copies ran while one was open for 3% of the time, Pallas kernels for 0%

commit v1 on v0

v1 whole, which is shorter than its diff:
```python
import functools

import jax
import jax.numpy as jnp
from jax import lax
from jax.experimental import pallas as pl
from jax.experimental.pallas import tpu as pltpu
from jax.sharding import PartitionSpec as P

MESH = pl.DeviceIdType.MESH
CHUNKS = 4


def kernel(
    ndp, n, sl,
    tok, cnt, gate_h, gi, up_h, ui, down_h, inv,
    out,
    gate, up, down, sendp, recvp, mine, sib, xs, hid, part, sibout, sibin, rsin, rsout, yexp, back,
    w_sem, x_s, x_r, ag_s, ag_r, sb_s, sb_r, ps_s, ps_r, rs_s, rs_r, bk_s, bk_r,
):
    f32, bf16 = jnp.float32, jnp.bfloat16
    rows_in, width = tok.shape
    bal = mine.shape[1]
    nj, knz = gi.shape
    bf = gate.shape[2]
    bd = down.shape[2]
    nblk = inv.shape[1]
    ndown = down.shape[0] - 1
    chunk = width // CHUNKS
    per_slab = rows_in // ndp
    d, m = lax.axis_index("dp"), lax.axis_index("mp")
    z, c = lax.div(m, 2), lax.rem(m, 2)
    twin = 2 * z + 1 - c

    def cols_of(q):
        return pl.ds(pl.multiple_of(q * chunk, chunk), chunk)

    def slab(s):
        return pl.ds(pl.multiple_of(s * sl, sl), sl)

    def loop(count, fn):
        def step(i, carry):
            fn(i)
            return carry
        lax.fori_loop(0, count, step, 0)

    def remote(src, dst, ssem, rsem, **where):
        return pltpu.make_async_remote_copy(
            src_ref=src, dst_ref=dst, send_sem=ssem, recv_sem=rsem, device_id=where, device_id_type=MESH
        )

    loads = [
        pltpu.make_async_copy(gate_h, gate, w_sem.at[0]),
        pltpu.make_async_copy(up_h, up, w_sem.at[1]),
        pltpu.make_async_copy(down_h, down.at[pl.ds(0, ndown)], w_sem.at[2]),
    ]

    barrier = pltpu.get_barrier_semaphore()
    for s in range(1, ndp):
        pl.semaphore_signal(barrier, inc=1, device_id={"dp": lax.rem(d + s, ndp)}, device_id_type=MESH)
    pl.semaphore_signal(barrier, inc=1, device_id={"mp": twin}, device_id_type=MESH)

    @pl.when(z > 0)
    def _():
        pl.semaphore_signal(barrier, inc=1, device_id={"mp": m - 2}, device_id_type=MESH)

    @pl.when(z < n - 1)
    def _():
        pl.semaphore_signal(barrier, inc=1, device_id={"mp": m + 2}, device_id_type=MESH)

    place = lax.broadcasted_iota(jnp.int32, (ndp * sl, rows_in), 0)
    slot = lax.broadcasted_iota(jnp.int32, (ndp * sl, rows_in), 1)
    inner = lax.rem(place, sl)
    perm = ((slot == inner * ndp + lax.div(place, sl)) & (inner < per_slab)).astype(f32).astype(bf16)
    place_t = lax.broadcasted_iota(jnp.int32, (rows_in, ndp * sl), 1)
    slot_t = lax.broadcasted_iota(jnp.int32, (rows_in, ndp * sl), 0)
    inner_t = lax.rem(place_t, sl)
    perm_t = ((slot_t == inner_t * ndp + lax.div(place_t, sl)) & (inner_t < per_slab)).astype(f32).astype(bf16)

    row = lax.broadcasted_iota(jnp.int32, (bal, ndp * sl), 0)
    col = lax.broadcasted_iota(jnp.int32, (bal, ndp * sl), 1)
    row_t = lax.broadcasted_iota(jnp.int32, (ndp * sl, bal), 1)
    col_t = lax.broadcasted_iota(jnp.int32, (ndp * sl, bal), 0)
    compact = jnp.zeros((bal, ndp * sl), f32)
    expand = jnp.zeros((ndp * sl, bal), f32)
    first = jnp.int32(0)
    for s in range(ndp):
        valid = lax.div(cnt[s, m], ndp)
        low, high = s * sl, s * sl + valid
        compact += ((col >= low) & (col < high) & (row == col - low + first)).astype(f32)
        expand += ((col_t >= low) & (col_t < high) & (row_t == col_t - low + first)).astype(f32)
        first = first + valid
    compact, expand = compact.astype(bf16), expand.astype(bf16)

    def exchange(src, dst, ssem, rsem, s, q):
        peer = lax.rem(d + s, ndp)
        return remote(src.at[slab(peer), cols_of(q)], dst.at[slab(d), cols_of(q)],
                      ssem.at[s - 1, q], rsem.at[s - 1, q], dp=peer)

    def arrived(src, dst, ssem, rsem, s, q):
        peer = lax.rem(d + ndp - s, ndp)
        return remote(src.at[slab(peer), cols_of(q)], dst.at[slab(peer), cols_of(q)],
                      ssem.at[s - 1, q], rsem.at[s - 1, q], dp=peer)

    def ag_copy(o, q, mp, send_slot):
        ref = mine.at[o, :, cols_of(q)]
        return remote(ref, ref, ag_s.at[send_slot, q], ag_r.at[o, q], mp=mp)

    def twin_copy(o, q):
        return remote(mine.at[o, :, cols_of(q)], sib.at[o, :, cols_of(q)], sb_s.at[o, q], sb_r.at[o, q], mp=twin)

    def part_copy(o, q):
        return remote(sibout.at[o, :, cols_of(q)], sibin.at[o, :, cols_of(q)], ps_s.at[o, q], ps_r.at[o, q], mp=twin)

    def rs_copy(t, q, mp, dst_slot):
        return remote(rsout.at[t, :, cols_of(q)], rsin.at[dst_slot, :, cols_of(q)],
                      rs_s.at[t, q], rs_r.at[dst_slot, q], mp=mp)

    at_end = (z == 0) | (z == n - 1)

    @pl.when(at_end)
    def _():
        pl.semaphore_wait(barrier, ndp + min(n - 1, 1))

    @pl.when(jnp.logical_not(at_end))
    def _():
        pl.semaphore_wait(barrier, ndp + 2)

    def send_tokens(q):
        cols = cols_of(q)
        sendp[:, cols] = jnp.dot(perm, tok[:, cols], preferred_element_type=f32).astype(bf16)
        for s in range(1, ndp):
            exchange(sendp, recvp, x_s, x_r, s, q).start()
        recvp[slab(d), cols] = sendp[slab(d), cols]
    loop(CHUNKS, send_tokens)
    for load in loads:
        load.start()
    down[ndown] = jnp.zeros(down.shape[1:], bf16)

    def spread(q):
        cols = cols_of(q)
        for s in range(1, ndp):
            arrived(sendp, recvp, x_s, x_r, s, q).wait_recv()
        mine[z, :, cols] = jnp.dot(compact, recvp[:, cols], preferred_element_type=f32).astype(bf16)

        @pl.when(z < n - 1)
        def _():
            ag_copy(z, q, m + 2, z).start()

        @pl.when(z > 0)
        def _():
            ag_copy(z, q, m - 2, n).start()
        twin_copy(z, q).start()
    loop(CHUNKS, spread)
    for load in loads:
        load.wait()

    def unit(o):
        def wait_rows(q):
            twin_copy(o, q).wait_recv()
        loop(CHUNKS, wait_rows)
        for b in range(nblk):
            xs[b, :bal, :] = mine[o, :, b * bd:(b + 1) * bd]
            xs[b, bal:, :] = sib[o, :, b * bd:(b + 1) * bd]

        def column(j):
            def picked(index):
                return jnp.concatenate([xs[index[j, k]] for k in range(knz)], axis=1)
            gv = jnp.dot(picked(gi), gate[j], preferred_element_type=f32)
            uv = jnp.dot(picked(ui), up[j], preferred_element_type=f32)
            hid[j] = (gv / (1.0 + jnp.exp(-gv)) * uv).astype(bf16)
        loop(nj, column)

        def down_chunk(q):
            def pair(i):
                b = q * (nblk // CHUNKS) + 2 * i
                acc = jnp.zeros((2 * bal, 2 * bd), f32)
                for j in range(nj):
                    w = jnp.concatenate([down[inv[j, b]], down[inv[j, b + 1]]], axis=1)
                    acc += jnp.dot(hid[j], w, preferred_element_type=f32)
                cols = pl.ds(pl.multiple_of(b * bd, 2 * bd), 2 * bd)
                part[o, :, cols] = acc[:bal]
                sibout[o, :, cols] = acc[bal:].astype(bf16)
            loop(nblk // CHUNKS // 2, pair)
            part_copy(o, q).start()
        loop(CHUNKS, down_chunk)

    def hop(tau, q):
        cols = cols_of(q)

        def pass_on(t, has_more, slot_in, mp):
            part_copy(t, q).wait_recv()
            acc = part[t, :, cols] + sibin[t, :, cols].astype(f32)

            @pl.when(has_more)
            def _():
                rs_copy(t, q, twin, slot_in).wait_recv()
                rsout[t, :, cols] = (acc + rsin[slot_in, :, cols].astype(f32)).astype(bf16)

            @pl.when(jnp.logical_not(has_more))
            def _():
                rsout[t, :, cols] = acc.astype(bf16)
            rs_copy(t, q, mp, slot_in).start()

        left = 2 * (n - 1) - z - tau

        @pl.when((left >= 0) & (left < z))
        def _():
            pass_on(left, z < n - 1, left, m - 2)
        right = tau - z

        @pl.when((right > z) & (right < n))
        def _():
            pass_on(right, z > 0, n + right, m + 2)

    def phase(tau):
        def forward(q):
            for sign in (-1, 1):
                o = z + sign * tau

                @pl.when((o >= 0) & (o < n) & (tau > 0))
                def _():
                    ag_copy(o, q, twin, o).wait_recv()
                    beyond = z - sign

                    @pl.when((beyond >= 0) & (beyond < n))
                    def _():
                        ag_copy(o, q, m - 2 * sign, o).start()
                    twin_copy(o, q).start()
        loop(CHUNKS, forward)

        def side(i):
            o = z + (2 * i - 1) * tau

            @pl.when((o >= 0) & (o < n) & ((tau > 0) | (i == 0)))
            def _():
                unit(o)
        loop(2, side)
        loop(CHUNKS, lambda q: hop(tau, q))
    loop(n, phase)

    def finish(q):
        cols = cols_of(q)
        loop(n - 1, lambda i: hop(n + i, q))
        part_copy(z, q).wait_recv()
        part[z, :, cols] = part[z, :, cols] + sibin[z, :, cols].astype(f32)

        @pl.when(z < n - 1)
        def _():
            rs_copy(z, q, twin, z).wait_recv()
            part[z, :, cols] = part[z, :, cols] + rsin[z, :, cols].astype(f32)

        @pl.when(z > 0)
        def _():
            rs_copy(z, q, twin, n + z).wait_recv()
            part[z, :, cols] = part[z, :, cols] + rsin[n + z, :, cols].astype(f32)
        total = part[z, :, cols].astype(bf16)
        yexp[:, cols] = jnp.dot(expand, total, preferred_element_type=f32).astype(bf16)
        for s in range(1, ndp):
            exchange(yexp, back, bk_s, bk_r, s, q).start()
        back[slab(d), cols] = yexp[slab(d), cols]
    loop(CHUNKS, finish)

    def store(q):
        cols = cols_of(q)
        for s in range(1, ndp):
            arrived(yexp, back, bk_s, bk_r, s, q).wait_recv()
        out[:, cols] = jnp.dot(perm_t, back[:, cols], preferred_element_type=f32).astype(bf16)
    loop(CHUNKS, store)

    def drain(q):
        for s in range(1, ndp):
            exchange(sendp, recvp, x_s, x_r, s, q).wait_send()
            exchange(yexp, back, bk_s, bk_r, s, q).wait_send()

        @pl.when(z > 0)
        def _():
            ag_copy(z, q, m - 2, n).wait_send()

        def each(o):
            twin_copy(o, q).wait_send()
            part_copy(o, q).wait_send()

            @pl.when(((o <= z) & (z < n - 1)) | ((o > z) & (z > 0)))
            def _():
                ag_copy(o, q, twin, o).wait_send()

            @pl.when(o != z)
            def _():
                rs_copy(o, q, twin, o).wait_send()
        loop(n, each)
    loop(CHUNKS, drain)


def body(tokens, row_counts, gate_blocks, gate_index, up_blocks, up_index, down_blocks, down_index):
    ndp, nmp = lax.axis_size("dp"), lax.axis_size("mp")
    n = nmp // 2
    rows_in, width = tokens.shape
    nj, knz, bd, bf = gate_blocks.shape
    nblk = width // bd
    bal = rows_in // 2
    sl = -(-(rows_in // ndp) // 16) * 16
    ids = jnp.arange(nj * knz, dtype=jnp.int32).reshape(nj, knz)
    hit = down_index[:, :, None] == jnp.arange(nblk, dtype=jnp.int32)
    inv = jnp.min(jnp.where(hit, ids[:, :, None], nj * knz), axis=1)
    bf16 = jnp.bfloat16
    vm, sm, hbm = (pl.BlockSpec(memory_space=s) for s in (pltpu.VMEM, pltpu.SMEM, pl.ANY))
    dma = pltpu.SemaphoreType.DMA
    rows = n * 2 * bal
    return pl.pallas_call(
        functools.partial(kernel, ndp, n, sl),
        out_shape=jax.ShapeDtypeStruct(tokens.shape, bf16),
        in_specs=[vm, sm, hbm, sm, hbm, sm, hbm, sm],
        out_specs=vm,
        scratch_shapes=[
            pltpu.VMEM((nj, knz * bd, bf), bf16),
            pltpu.VMEM((nj, knz * bd, bf), bf16),
            pltpu.VMEM((nj * knz + 1, bf, bd), bf16),
            pltpu.VMEM((ndp * sl, width), bf16),
            pltpu.VMEM((ndp * sl, width), bf16),
            pltpu.VMEM((n, bal, width), bf16),
            pltpu.VMEM((n, bal, width), bf16),
            pltpu.VMEM((nblk, 2 * bal, bd), bf16),
            pltpu.VMEM((nj, 2 * bal, bf), bf16),
            pltpu.VMEM((n, bal, width), jnp.float32),
            pltpu.VMEM((n, bal, width), bf16),
            pltpu.VMEM((n, bal, width), bf16),
            pltpu.VMEM((2 * n, bal, width), bf16),
            pltpu.VMEM((n, bal, width), bf16),
            pltpu.VMEM((ndp * sl, width), bf16),
            pltpu.VMEM((ndp * sl, width), bf16),
            dma((3,)),
            dma((ndp - 1, CHUNKS)), dma((ndp - 1, CHUNKS)),
            dma((n + 1, CHUNKS)), dma((n, CHUNKS)),
            dma((n, CHUNKS)), dma((n, CHUNKS)),
            dma((n, CHUNKS)), dma((n, CHUNKS)),
            dma((n, CHUNKS)), dma((2 * n, CHUNKS)),
            dma((ndp - 1, CHUNKS)), dma((ndp - 1, CHUNKS)),
        ],
        compiler_params=pltpu.CompilerParams(
            collective_id=0, has_side_effects=True, vmem_limit_bytes=60 * 1024 * 1024
        ),
        cost_estimate=pl.CostEstimate(
            flops=6 * rows * nj * knz * bd * bf, bytes_accessed=6 * nj * knz * bd * bf, transcendentals=rows * nj * bf
        ),
    )(
        tokens, row_counts, gate_blocks.reshape(nj, knz * bd, bf), gate_index,
        up_blocks.reshape(nj, knz * bd, bf), up_index, down_blocks.reshape(nj * knz, bf, bd), inv,
    )


def solution(mesh):
    in_specs = (
        P(("dp", "mp"), None),
        P(),
        P("mp", None, None, None),
        P("mp", None),
        P("mp", None, None, None),
        P("mp", None),
        P("mp", None, None, None),
        P("mp", None),
    )
    out_specs = P(("dp", "mp"), None)
    return jax.shard_map(body, mesh=mesh, in_specs=in_specs, out_specs=out_specs, check_vma=False)
```

time: 263 us -> 131 us (0.50)
  Pallas kernels: 0 us -> 128 us
  waiting for transfers between devices: 103 us -> 0 us
  other arithmetic: 52.2 us -> 1.4 us
  local copies, waits for them, and re-layouts: 50.8 us -> 2.26 us
  matrix products: 21.8 us -> 0 us
  blocking collectives: 15.4 us -> 0 us
  between operations: 13.5 us -> 0.01 us
  starting transfers between devices: 5.39 us -> 0 us
    pallas_call x0 -> x1, Pallas kernels: none -> 128 us  [body(): pl.pallas_call(functools.partial(kernel, ndp, n, sl), out_shape=jax.Shape...]
    reduce_scatter x1 -> x0, waiting for transfers between devices: 48.8 us -> none  [body(): lax.psum_scatter(apply_down(hidden_all, down_blocks, down_index, block_to...]
    all_gather x1 -> x0, waiting for transfers between devices: 47.1 us -> none  [body(): lax.all_gather(chosen_rows, 'mp', axis=0, tiled=True)]
    scatter-add x1 -> x0, other arithmetic: 39 us -> none  [apply_down(): placed = placed.at[:, down_index.reshape(-1)].add(flat_products)]
    dot_general x2 -> x0, matrix products: 21.8 us -> none  [the longest x1 14.1 us: apply_down(): jnp.einsum('rjn,jknc->rjkc', hidden_split, down_blocks, preferred_element...]
    gather x4 -> x0, local copies, waits for them, and re-layouts: 19 us -> none  [the longest x1 8.74 us: make_hidden(): up_input = jnp.take(split_rows, up_index, axis=1)]
    all_to_all x1 -> x0, blocking collectives: 15.4 us -> none  [body(): lax.all_to_all(returned.reshape(slot_rows, dp_size, model_width), 'dp', s...]
    reshape x8 -> x0, local copies, waits for them, and re-layouts: 10.9 us -> none  [the longest x1 5.35 us: make_hidden(): split_rows = row_block.reshape(row_count, -1, block_width)]
  transfers between devices with their start and end apart: 3 -> 0, of which waited for: 3 -> 0; matrix products, arithmetic and copies ran while one was open for 3% -> 0% of each run, Pallas kernels for 0% -> 0%
where the time goes in v1:
time: 131 us
  Pallas kernels  128 us (98%)
  local copies, waits for them, and re-layouts  2.26 us (2%)
  other arithmetic  1.4 us (1%)
    pallas_call x1, Pallas kernels, body(): pl.pallas_call(functools.partial(kernel, ndp, n, sl), out_shape=jax.Shape...  128 us

profile of v1, /device:TPU:0, one launch (start us, length us, event | category | flops | bytes accessed | tf_op | source)
XLA Modules:
  0.0 131.3 jit_solution(8885171943483896822)
XLA Ops:
  0.0 1.4 %select_reduce_fusion.inv = s32[8,64]{1,0:T(8,128)} fusion(s32[8,16]{1,0:T(8,128)S(1)} %multiply_add_fusion, s32[8,16]{1,0:T(8,128)} %param.15), kind=kLoop, calls=%fused_computation | loop fusion | flops 24064 | bytes 3072 | tf_op jit(solution)/shard_map/reduce_min | solution.py:305
  1.4 127.6 %shard_map.82 = bf16[64,8192]{1,0:T(8,128)(2,1)} custom-call(bf16[64,8192]{1,0:T(8,128)(2,1)} %tok.1, s32[4,8]{1,0:T(4,128)} %cnt.1, bf16[8,2048,256]{2,1,0:T(8,128)(2,1)} %bitcast.3, s32[8,16]{1,0:T(8,128)} %gi.1, bf16[8,2048,256]{2,1,0:T(8,128)(2,1)} %bitcast.4, s32[8,16]{1,0:T(8,128)} %ui.1, bf16[128,256,128]{2,1,0:T(8,128)(2,1)} %bitcast.5, ...), custom_call_target="tpu_custom_call" | custom-call | flops 6442450944 | bytes 25165824 | tf_op jit(solution)/shard_map/pallas_call | solution.py:310
  129.0 2.3 %copy.10 = bf16[64,8192]{1,0:T(8,128)(2,1)} copy(bf16[64,8192]{1,0:T(8,128)(2,1)} %shard_map.82) | data formatting | bytes 2097152
  (1 shorter events, 0.0 us)

commit v2 on v1

--- a/solution.py
+++ b/solution.py
@@ -15,7 +15,7 @@
     ndp, n, sl,
     tok, cnt, gate_h, gi, up_h, ui, down_h, inv,
     out,
-    gate, up, down, sendp, recvp, mine, sib, xs, hid, part, sibout, sibin, rsin, rsout, yexp, back,
+    gate, up, down, sendp, recvp, mine, sib, xs, hid, prod, total, part, sibout, sibin, rsin, rsout, yexp, back,
     w_sem, x_s, x_r, ag_s, ag_r, sb_s, sb_r, ps_s, ps_r, rs_s, rs_r, bk_s, bk_r,
 ):
     f32, bf16 = jnp.float32, jnp.bfloat16
@@ -25,7 +25,7 @@
     bf = gate.shape[2]
     bd = down.shape[2]
     nblk = inv.shape[1]
-    ndown = down.shape[0] - 1
+    ndown = down.shape[0]
     chunk = width // CHUNKS
     per_slab = rows_in // ndp
     d, m = lax.axis_index("dp"), lax.axis_index("mp")
@@ -52,7 +52,7 @@
     loads = [
         pltpu.make_async_copy(gate_h, gate, w_sem.at[0]),
         pltpu.make_async_copy(up_h, up, w_sem.at[1]),
-        pltpu.make_async_copy(down_h, down.at[pl.ds(0, ndown)], w_sem.at[2]),
+        pltpu.make_async_copy(down_h, down, w_sem.at[2]),
     ]
 
     barrier = pltpu.get_barrier_semaphore()
@@ -135,7 +135,7 @@
     loop(CHUNKS, send_tokens)
     for load in loads:
         load.start()
-    down[ndown] = jnp.zeros(down.shape[1:], bf16)
+    prod[ndown] = jnp.zeros(prod.shape[1:], f32)
 
     def spread(q):
         cols = cols_of(q)
@@ -155,7 +155,26 @@
     for load in loads:
         load.wait()
 
-    def unit(o):
+    def take(o, q, sign):
+        ag_copy(o, q, twin, o).wait_recv()
+        beyond = z - sign
+
+        @pl.when((beyond >= 0) & (beyond < n))
+        def _():
+            ag_copy(o, q, m - 2 * sign, o).start()
+        twin_copy(o, q).start()
+
+    def take_all(tau, q, passing):
+        for sign in (-1, 1):
+            o, beyond = z + sign * tau, z - sign
+            inside = (beyond >= 0) & (beyond < n)
+            wanted = inside if passing else jnp.logical_not(inside)
+
+            @pl.when((o >= 0) & (o < n) & (tau > 0) & wanted)
+            def _():
+                take(o, q, sign)
+
+    def unit(o, tau, last):
         def wait_rows(q):
             twin_copy(o, q).wait_recv()
         loop(CHUNKS, wait_rows)
@@ -163,34 +182,52 @@
             xs[b, :bal, :] = mine[o, :, b * bd:(b + 1) * bd]
             xs[b, bal:, :] = sib[o, :, b * bd:(b + 1) * bd]
 
-        def column(j):
-            def picked(index):
-                return jnp.concatenate([xs[index[j, k]] for k in range(knz)], axis=1)
-            gv = jnp.dot(picked(gi), gate[j], preferred_element_type=f32)
-            uv = jnp.dot(picked(ui), up[j], preferred_element_type=f32)
-            hid[j] = (gv / (1.0 + jnp.exp(-gv)) * uv).astype(bf16)
-        loop(nj, column)
-
-        def down_chunk(q):
-            def pair(i):
-                b = q * (nblk // CHUNKS) + 2 * i
-                acc = jnp.zeros((2 * bal, 2 * bd), f32)
-                for j in range(nj):
-                    w = jnp.concatenate([down[inv[j, b]], down[inv[j, b + 1]]], axis=1)
-                    acc += jnp.dot(hid[j], w, preferred_element_type=f32)
-                cols = pl.ds(pl.multiple_of(b * bd, 2 * bd), 2 * bd)
-                part[o, :, cols] = acc[:bal]
-                sibout[o, :, cols] = acc[bal:].astype(bf16)
-            loop(nblk // CHUNKS // 2, pair)
+        group = nj // CHUNKS
+
+        def columns(q):
+            for i in range(group):
+                j = q * group + i
+
+                def picked(index):
+                    return jnp.concatenate([xs[index[j, k]] for k in range(knz)], axis=1)
+                gv = jnp.dot(picked(gi), gate[j], preferred_element_type=f32)
+                uv = jnp.dot(picked(ui), up[j], preferred_element_type=f32)
+                hid[j] = (gv / (1.0 + jnp.exp(-gv)) * uv).astype(bf16)
+
+            @pl.when(last)
+            def _():
+                take_all(tau + 1, q, True)
+        loop(CHUNKS, columns)
+
+        def down_row(j):
+            h = hid[j]
+            for i in range(0, knz, 2):
+                w = jnp.concatenate([down[j * knz + i], down[j * knz + i + 1]], axis=1)
+                p = jnp.dot(h, w, preferred_element_type=f32)
+                prod[j * knz + i] = p[:, :bd]
+                prod[j * knz + i + 1] = p[:, bd:]
+        loop(nj, down_row)
+
+        def gather(q):
+            def some(i):
+                for e in range(4):
+                    b = q * (nblk // CHUNKS) + 4 * i + e
+                    acc = prod[inv[0, b]]
+                    for j in range(1, nj):
+                        acc += prod[inv[j, b]]
+                    cols = pl.ds(pl.multiple_of(b * bd, bd), bd)
+                    part[o, :, cols] = acc[:bal].astype(bf16)
+                    sibout[o, :, cols] = acc[bal:].astype(bf16)
+            loop(nblk // CHUNKS // 4, some)
             part_copy(o, q).start()
-        loop(CHUNKS, down_chunk)
+        loop(CHUNKS, gather)
 
     def hop(tau, q):
         cols = cols_of(q)
 
         def pass_on(t, has_more, slot_in, mp):
             part_copy(t, q).wait_recv()
-            acc = part[t, :, cols] + sibin[t, :, cols].astype(f32)
+            acc = part[t, :, cols].astype(f32) + sibin[t, :, cols].astype(f32)
 
             @pl.when(has_more)
             def _():
@@ -214,27 +251,14 @@
             pass_on(right, z > 0, n + right, m + 2)
 
     def phase(tau):
-        def forward(q):
-            for sign in (-1, 1):
-                o = z + sign * tau
-
-                @pl.when((o >= 0) & (o < n) & (tau > 0))
-                def _():
-                    ag_copy(o, q, twin, o).wait_recv()
-                    beyond = z - sign
-
-                    @pl.when((beyond >= 0) & (beyond < n))
-                    def _():
-                        ag_copy(o, q, m - 2 * sign, o).start()
-                    twin_copy(o, q).start()
-        loop(CHUNKS, forward)
+        loop(CHUNKS, lambda q: take_all(tau, q, False))
 
         def side(i):
             o = z + (2 * i - 1) * tau
 
             @pl.when((o >= 0) & (o < n) & ((tau > 0) | (i == 0)))
             def _():
-                unit(o)
+                unit(o, tau, (i == 1) | (tau == 0) | (z + tau >= n))
         loop(2, side)
         loop(CHUNKS, lambda q: hop(tau, q))
     loop(n, phase)
@@ -243,19 +267,18 @@
         cols = cols_of(q)
         loop(n - 1, lambda i: hop(n + i, q))
         part_copy(z, q).wait_recv()
-        part[z, :, cols] = part[z, :, cols] + sibin[z, :, cols].astype(f32)
+        total[...] = part[z, :, cols].astype(f32) + sibin[z, :, cols].astype(f32)
 
         @pl.when(z < n - 1)
         def _():
             rs_copy(z, q, twin, z).wait_recv()
-            part[z, :, cols] = part[z, :, cols] + rsin[z, :, cols].astype(f32)
+            total[...] += rsin[z, :, cols].astype(f32)
 
         @pl.when(z > 0)
         def _():
             rs_copy(z, q, twin, n + z).wait_recv()
-            part[z, :, cols] = part[z, :, cols] + rsin[n + z, :, cols].astype(f32)
-        total = part[z, :, cols].astype(bf16)
-        yexp[:, cols] = jnp.dot(expand, total, preferred_element_type=f32).astype(bf16)
+            total[...] += rsin[n + z, :, cols].astype(f32)
+        yexp[:, cols] = jnp.dot(expand, total[...].astype(bf16), preferred_element_type=f32).astype(bf16)
         for s in range(1, ndp):
             exchange(yexp, back, bk_s, bk_r, s, q).start()
         back[slab(d), cols] = yexp[slab(d), cols]
@@ -315,14 +338,16 @@
         scratch_shapes=[
             pltpu.VMEM((nj, knz * bd, bf), bf16),
             pltpu.VMEM((nj, knz * bd, bf), bf16),
-            pltpu.VMEM((nj * knz + 1, bf, bd), bf16),
+            pltpu.VMEM((nj * knz, bf, bd), bf16),
             pltpu.VMEM((ndp * sl, width), bf16),
             pltpu.VMEM((ndp * sl, width), bf16),
             pltpu.VMEM((n, bal, width), bf16),
             pltpu.VMEM((n, bal, width), bf16),
             pltpu.VMEM((nblk, 2 * bal, bd), bf16),
             pltpu.VMEM((nj, 2 * bal, bf), bf16),
-            pltpu.VMEM((n, bal, width), jnp.float32),
+            pltpu.VMEM((nj * knz + 1, 2 * bal, bd), jnp.float32),
+            pltpu.VMEM((bal, width // CHUNKS), jnp.float32),
+            pltpu.VMEM((n, bal, width), bf16),
             pltpu.VMEM((n, bal, width), bf16),
             pltpu.VMEM((n, bal, width), bf16),
             pltpu.VMEM((2 * n, bal, width), bf16),

time: 131 us -> 98.3 us (0.75)
  Pallas kernels: 128 us -> 94.4 us
    pallas_call x1, Pallas kernels: 128 us -> 94.4 us  [body(): pl.pallas_call(functools.partial(kernel, ndp, n, sl), out_shape=jax.Shape...]
where the time goes in v2:
time: 98.3 us; the launch traced here: 98.1 us
  Pallas kernels  94.4 us (96%)
  local copies, waits for them, and re-layouts  2.26 us (2%)
  other arithmetic  1.4 us (1%)
    pallas_call x1, Pallas kernels, body(): pl.pallas_call(functools.partial(kernel, ndp, n, sl), out_shape=jax.Shape...  94.4 us
    unnamed x1, local copies, waits for them, and re-layouts  2.26 us

profile of v2, /device:TPU:0, one launch (start us, length us, event | category | flops | bytes accessed | tf_op | source)
XLA Modules:
  0.0 98.1 jit_solution(16780297191531183420)
XLA Ops:
  0.0 1.4 %select_reduce_fusion.inv = s32[8,64]{1,0:T(8,128)} fusion(s32[8,16]{1,0:T(8,128)S(1)} %multiply_add_fusion, s32[8,16]{1,0:T(8,128)} %param.15), kind=kLoop, calls=%fused_computation | loop fusion | flops 24064 | bytes 3072 | tf_op jit(solution)/shard_map/reduce_min | solution.py:328
  1.4 94.4 %shard_map.82 = bf16[64,8192]{1,0:T(8,128)(2,1)} custom-call(bf16[64,8192]{1,0:T(8,128)(2,1)} %tok.1, s32[4,8]{1,0:T(4,128)} %cnt.1, bf16[8,2048,256]{2,1,0:T(8,128)(2,1)} %bitcast.3, s32[8,16]{1,0:T(8,128)} %gi.1, bf16[8,2048,256]{2,1,0:T(8,128)(2,1)} %bitcast.4, s32[8,16]{1,0:T(8,128)} %ui.1, bf16[128,256,128]{2,1,0:T(8,128)(2,1)} %bitcast.5, ...), custom_call_target="tpu_custom_call" | custom-call | flops 6442450944 | bytes 25165824 | tf_op jit(solution)/shard_map/pallas_call | solution.py:333
  95.8 2.3 %copy.10 = bf16[64,8192]{1,0:T(8,128)(2,1)} copy(bf16[64,8192]{1,0:T(8,128)(2,1)} %shard_map.82) | data formatting | bytes 2097152
  (1 shorter events, 0.0 us)

commit v3 on v2

--- a/solution.py
+++ b/solution.py
@@ -15,7 +15,7 @@
     ndp, n, sl,
     tok, cnt, gate_h, gi, up_h, ui, down_h, inv,
     out,
-    gate, up, down, sendp, recvp, mine, sib, xs, hid, prod, total, part, sibout, sibin, rsin, rsout, yexp, back,
+    gate, up, down, sendp, recvp, mine, sib, xs, hid, prod, total, part, sibout, sibin, rsin, back,
     w_sem, x_s, x_r, ag_s, ag_r, sb_s, sb_r, ps_s, ps_r, rs_s, rs_r, bk_s, bk_r,
 ):
     f32, bf16 = jnp.float32, jnp.bfloat16
@@ -113,7 +113,7 @@
         return remote(sibout.at[o, :, cols_of(q)], sibin.at[o, :, cols_of(q)], ps_s.at[o, q], ps_r.at[o, q], mp=twin)
 
     def rs_copy(t, q, mp, dst_slot):
-        return remote(rsout.at[t, :, cols_of(q)], rsin.at[dst_slot, :, cols_of(q)],
+        return remote(part.at[t, :, cols_of(q)], rsin.at[dst_slot, :, cols_of(q)],
                       rs_s.at[t, q], rs_r.at[dst_slot, q], mp=mp)
 
     at_end = (z == 0) | (z == n - 1)
@@ -135,25 +135,7 @@
     loop(CHUNKS, send_tokens)
     for load in loads:
         load.start()
-    prod[ndown] = jnp.zeros(prod.shape[1:], f32)
-
-    def spread(q):
-        cols = cols_of(q)
-        for s in range(1, ndp):
-            arrived(sendp, recvp, x_s, x_r, s, q).wait_recv()
-        mine[z, :, cols] = jnp.dot(compact, recvp[:, cols], preferred_element_type=f32).astype(bf16)
-
-        @pl.when(z < n - 1)
-        def _():
-            ag_copy(z, q, m + 2, z).start()
-
-        @pl.when(z > 0)
-        def _():
-            ag_copy(z, q, m - 2, n).start()
-        twin_copy(z, q).start()
-    loop(CHUNKS, spread)
-    for load in loads:
-        load.wait()
+    prod[ndown] = jnp.zeros(prod.shape[1:], bf16)
 
     def take(o, q, sign):
         ag_copy(o, q, twin, o).wait_recv()
@@ -170,56 +152,92 @@
             inside = (beyond >= 0) & (beyond < n)
             wanted = inside if passing else jnp.logical_not(inside)
 
-            @pl.when((o >= 0) & (o < n) & (tau > 0) & wanted)
+            @pl.when((o >= 0) & (o < n) & wanted)
             def _():
                 take(o, q, sign)
 
-    def unit(o, tau, last):
+    def spread(q):
+        cols = cols_of(q)
+        for s in range(1, ndp):
+            arrived(sendp, recvp, x_s, x_r, s, q).wait_recv()
+        mine[z, :, cols] = jnp.dot(compact, recvp[:, cols], preferred_element_type=f32).astype(bf16)
+
+        @pl.when(z < n - 1)
+        def _():
+            ag_copy(z, q, m + 2, z).start()
+
+        @pl.when(z > 0)
+        def _():
+            ag_copy(z, q, m - 2, n).start()
+        twin_copy(z, q).start()
+
+        @pl.when(q > 0)
+        def _():
+            take_all(1, q - 1, True)
+            take_all(1, q - 1, False)
+    loop(CHUNKS, spread)
+    take_all(1, CHUNKS - 1, True)
+    take_all(1, CHUNKS - 1, False)
+    for load in loads:
+        load.wait()
+
+    def unit(origins, tau, last):
+        rows = pl.ds(0, 2 * bal * len(origins))
+
         def wait_rows(q):
-            twin_copy(o, q).wait_recv()
+            for o in origins:
+                twin_copy(o, q).wait_recv()
         loop(CHUNKS, wait_rows)
-        for b in range(nblk):
-            xs[b, :bal, :] = mine[o, :, b * bd:(b + 1) * bd]
-            xs[b, bal:, :] = sib[o, :, b * bd:(b + 1) * bd]
-
-        group = nj // CHUNKS
-
-        def columns(q):
+        for i, o in enumerate(origins):
+            top = 2 * bal * i
+            for b in range(nblk):
+                xs[b, top:top + bal, :] = mine[o, :, b * bd:(b + 1) * bd]
+                xs[b, top + bal:top + 2 * bal, :] = sib[o, :, b * bd:(b + 1) * bd]
+
+        steps = min(nj, CHUNKS)
+        group, passes = nj // steps, CHUNKS // steps
+
+        def columns(g):
             for i in range(group):
-                j = q * group + i
+                j = g * group + i
 
                 def picked(index):
-                    return jnp.concatenate([xs[index[j, k]] for k in range(knz)], axis=1)
+                    return jnp.concatenate([xs[index[j, k], rows, :] for k in range(knz)], axis=1)
                 gv = jnp.dot(picked(gi), gate[j], preferred_element_type=f32)
                 uv = jnp.dot(picked(ui), up[j], preferred_element_type=f32)
-                hid[j] = (gv / (1.0 + jnp.exp(-gv)) * uv).astype(bf16)
-
-            @pl.when(last)
-            def _():
-                take_all(tau + 1, q, True)
-        loop(CHUNKS, columns)
+                hid[j, rows, :] = (gv / (1.0 + jnp.exp(-gv)) * uv).astype(bf16)
+            if last is not None:
+                @pl.when(last)
+                def _():
+                    for i in range(passes):
+                        take_all(tau + 1, g * passes + i, True)
+        loop(steps, columns)
 
         def down_row(j):
-            h = hid[j]
-            for i in range(0, knz, 2):
-                w = jnp.concatenate([down[j * knz + i], down[j * knz + i + 1]], axis=1)
-                p = jnp.dot(h, w, preferred_element_type=f32)
-                prod[j * knz + i] = p[:, :bd]
-                prod[j * knz + i + 1] = p[:, bd:]
+            h = hid[j, rows, :]
+            for i in range(0, knz, 4):
+                w = jnp.concatenate([down[j * knz + i + e] for e in range(4)], axis=1)
+                p = jnp.dot(h, w, preferred_element_type=f32).astype(bf16)
+                for e in range(4):
+                    prod[j * knz + i + e, rows, :] = p[:, e * bd:(e + 1) * bd]
         loop(nj, down_row)
 
         def gather(q):
             def some(i):
-                for e in range(4):
-                    b = q * (nblk // CHUNKS) + 4 * i + e
-                    acc = prod[inv[0, b]]
+                for e in range(2):
+                    b = q * (nblk // CHUNKS) + 2 * i + e
+                    acc = prod[inv[0, b], rows, :].astype(f32)
                     for j in range(1, nj):
-                        acc += prod[inv[j, b]]
+                        acc += prod[inv[j, b], rows, :].astype(f32)
                     cols = pl.ds(pl.multiple_of(b * bd, bd), bd)
-                    part[o, :, cols] = acc[:bal].astype(bf16)
-                    sibout[o, :, cols] = acc[bal:].astype(bf16)
-            loop(nblk // CHUNKS // 4, some)
-            part_copy(o, q).start()
+                    acc = acc.astype(bf16)
+                    for r, o in enumerate(origins):
+                        top = 2 * bal * r
+                        part[o, :, cols] = acc[top:top + bal]
+                        sibout[o, :, cols] = acc[top + bal:top + 2 * bal]
+            loop(nblk // CHUNKS // 2, some)
+            for o in origins:
+                part_copy(o, q).start()
         loop(CHUNKS, gather)
 
     def hop(tau, q):
@@ -232,11 +250,11 @@
             @pl.when(has_more)
             def _():
                 rs_copy(t, q, twin, slot_in).wait_recv()
-                rsout[t, :, cols] = (acc + rsin[slot_in, :, cols].astype(f32)).astype(bf16)
+                part[t, :, cols] = (acc + rsin[slot_in, :, cols].astype(f32)).astype(bf16)
 
             @pl.when(jnp.logical_not(has_more))
             def _():
-                rsout[t, :, cols] = acc.astype(bf16)
+                part[t, :, cols] = acc.astype(bf16)
             rs_copy(t, q, mp, slot_in).start()
 
         left = 2 * (n - 1) - z - tau
@@ -250,21 +268,37 @@
         def _():
             pass_on(right, z > 0, n + right, m + 2)
 
-    def phase(tau):
+    def near(i):
+        o = z + 2 * i - 1
+
+        @pl.when(at_end & (o >= 0) & (o < n))
+        def _():
+            unit([z, o], 1, None)
+    loop(2, near)
+    if n > 2:
+        @pl.when(jnp.logical_not(at_end))
+        def _():
+            unit([z, z - 1, z + 1], 1, z >= 0)
+    loop(CHUNKS, lambda q: hop(1, q))
+
+    def phase(i):
+        tau = i + 2
         loop(CHUNKS, lambda q: take_all(tau, q, False))
 
         def side(i):
             o = z + (2 * i - 1) * tau
 
-            @pl.when((o >= 0) & (o < n) & ((tau > 0) | (i == 0)))
-            def _():
-                unit(o, tau, (i == 1) | (tau == 0) | (z + tau >= n))
+            @pl.when((o >= 0) & (o < n))
+            def _():
+                unit([o], tau, (i == 1) | (z + tau >= n))
         loop(2, side)
         loop(CHUNKS, lambda q: hop(tau, q))
-    loop(n, phase)
+    loop(n - 2, phase)
 
     def finish(q):
         cols = cols_of(q)
+        for s in range(1, ndp):
+            exchange(sendp, recvp, x_s, x_r, s, q).wait_send()
         loop(n - 1, lambda i: hop(n + i, q))
         part_copy(z, q).wait_recv()
         total[...] = part[z, :, cols].astype(f32) + sibin[z, :, cols].astype(f32)
@@ -278,23 +312,22 @@
         def _():
             rs_copy(z, q, twin, n + z).wait_recv()
             total[...] += rsin[n + z, :, cols].astype(f32)
-        yexp[:, cols] = jnp.dot(expand, total[...].astype(bf16), preferred_element_type=f32).astype(bf16)
-        for s in range(1, ndp):
-            exchange(yexp, back, bk_s, bk_r, s, q).start()
-        back[slab(d), cols] = yexp[slab(d), cols]
+        sendp[:, cols] = jnp.dot(expand, total[...].astype(bf16), preferred_element_type=f32).astype(bf16)
+        for s in range(1, ndp):
+            exchange(sendp, back, bk_s, bk_r, s, q).start()
+        back[slab(d), cols] = sendp[slab(d), cols]
     loop(CHUNKS, finish)
 
     def store(q):
         cols = cols_of(q)
         for s in range(1, ndp):
-            arrived(yexp, back, bk_s, bk_r, s, q).wait_recv()
+            arrived(sendp, back, bk_s, bk_r, s, q).wait_recv()
         out[:, cols] = jnp.dot(perm_t, back[:, cols], preferred_element_type=f32).astype(bf16)
     loop(CHUNKS, store)
 
     def drain(q):
         for s in range(1, ndp):
-            exchange(sendp, recvp, x_s, x_r, s, q).wait_send()
-            exchange(yexp, back, bk_s, bk_r, s, q).wait_send()
+            exchange(sendp, back, bk_s, bk_r, s, q).wait_send()
 
         @pl.when(z > 0)
         def _():
@@ -330,6 +363,7 @@
     vm, sm, hbm = (pl.BlockSpec(memory_space=s) for s in (pltpu.VMEM, pltpu.SMEM, pl.ANY))
     dma = pltpu.SemaphoreType.DMA
     rows = n * 2 * bal
+    tall = 2 * bal * min(n, 3)
     return pl.pallas_call(
         functools.partial(kernel, ndp, n, sl),
         out_shape=jax.ShapeDtypeStruct(tokens.shape, bf16),
@@ -343,16 +377,14 @@
             pltpu.VMEM((ndp * sl, width), bf16),
             pltpu.VMEM((n, bal, width), bf16),
             pltpu.VMEM((n, bal, width), bf16),
-            pltpu.VMEM((nblk, 2 * bal, bd), bf16),
-            pltpu.VMEM((nj, 2 * bal, bf), bf16),
-            pltpu.VMEM((nj * knz + 1, 2 * bal, bd), jnp.float32),
+            pltpu.VMEM((nblk, tall, bd), bf16),
+            pltpu.VMEM((nj, tall, bf), bf16),
+            pltpu.VMEM((nj * knz + 1, tall, bd), bf16),
             pltpu.VMEM((bal, width // CHUNKS), jnp.float32),
             pltpu.VMEM((n, bal, width), bf16),
             pltpu.VMEM((n, bal, width), bf16),
             pltpu.VMEM((n, bal, width), bf16),
             pltpu.VMEM((2 * n, bal, width), bf16),
-            pltpu.VMEM((n, bal, width), bf16),
-            pltpu.VMEM((ndp * sl, width), bf16),
             pltpu.VMEM((ndp * sl, width), bf16),
             dma((3,)),
             dma((ndp - 1, CHUNKS)), dma((ndp - 1, CHUNKS)),

time: 98.3 us -> 102 us (1.038)
  Pallas kernels: 94.4 us -> 98.1 us
    pallas_call x1, Pallas kernels: 94.4 us -> 98.1 us  [body(): pl.pallas_call(functools.partial(kernel, ndp, n, sl), out_shape=jax.Shape...]
where the time goes in v3:
time: 102 us
  Pallas kernels  98.1 us (96%)
  local copies, waits for them, and re-layouts  2.26 us (2%)
  other arithmetic  1.4 us (1%)
    pallas_call x1, Pallas kernels, body(): pl.pallas_call(functools.partial(kernel, ndp, n, sl), out_shape=jax.Shape...  98.1 us
    unnamed x1, local copies, waits for them, and re-layouts  2.26 us

profile of v3, /device:TPU:0, one launch (start us, length us, event | category | flops | bytes accessed | tf_op | source)
XLA Modules:
  0.0 101.7 jit_solution(10263088577803984488)
XLA Ops:
  0.0 1.4 %select_reduce_fusion.inv = s32[8,64]{1,0:T(8,128)} fusion(s32[8,16]{1,0:T(8,128)S(1)} %multiply_add_fusion, s32[8,16]{1,0:T(8,128)} %param.15), kind=kLoop, calls=%fused_computation | loop fusion | flops 24064 | bytes 3072 | tf_op jit(solution)/shard_map/reduce_min | solution.py:361
  1.4 98.1 %shard_map.82 = bf16[64,8192]{1,0:T(8,128)(2,1)} custom-call(bf16[64,8192]{1,0:T(8,128)(2,1)} %tok.1, s32[4,8]{1,0:T(4,128)} %cnt.1, bf16[8,2048,256]{2,1,0:T(8,128)(2,1)} %bitcast.3, s32[8,16]{1,0:T(8,128)} %gi.1, bf16[8,2048,256]{2,1,0:T(8,128)(2,1)} %bitcast.4, s32[8,16]{1,0:T(8,128)} %ui.1, bf16[128,256,128]{2,1,0:T(8,128)(2,1)} %bitcast.5, ...), custom_call_target="tpu_custom_call" | custom-call | flops 6442450944 | bytes 25165824 | tf_op jit(solution)/shard_map/pallas_call | solution.py:367
  99.5 2.3 %copy.10 = bf16[64,8192]{1,0:T(8,128)(2,1)} copy(bf16[64,8192]{1,0:T(8,128)(2,1)} %shard_map.82) | data formatting | bytes 2097152
  (1 shorter events, 0.0 us)

commit v4 on v3

--- a/solution.py
+++ b/solution.py
@@ -8,7 +8,7 @@
 from jax.sharding import PartitionSpec as P
 
 MESH = pl.DeviceIdType.MESH
-CHUNKS = 4
+CHUNKS = 8
 
 
 def kernel(
@@ -135,7 +135,7 @@
     loop(CHUNKS, send_tokens)
     for load in loads:
         load.start()
-    prod[ndown] = jnp.zeros(prod.shape[1:], bf16)
+    prod[ndown] = jnp.zeros(prod.shape[1:], f32)
 
     def take(o, q, sign):
         ag_copy(o, q, twin, o).wait_recv()
@@ -180,6 +180,34 @@
     take_all(1, CHUNKS - 1, False)
     for load in loads:
         load.wait()
+
+    def hop(tau, q):
+        cols = cols_of(q)
+
+        def pass_on(t, has_more, slot_in, mp):
+            part_copy(t, q).wait_recv()
+            acc = part[t, :, cols].astype(f32) + sibin[t, :, cols].astype(f32)
+
+            @pl.when(has_more)
+            def _():
+                rs_copy(t, q, twin, slot_in).wait_recv()
+                part[t, :, cols] = (acc + rsin[slot_in, :, cols].astype(f32)).astype(bf16)
+
+            @pl.when(jnp.logical_not(has_more))
+            def _():
+                part[t, :, cols] = acc.astype(bf16)
+            rs_copy(t, q, mp, slot_in).start()
+
+        left = 2 * (n - 1) - z - tau
+
+        @pl.when((left >= 0) & (left < z))
+        def _():
+            pass_on(left, z < n - 1, left, m - 2)
+        right = tau - z
+
+        @pl.when((right > z) & (right < n))
+        def _():
+            pass_on(right, z > 0, n + right, m + 2)
 
     def unit(origins, tau, last):
         rows = pl.ds(0, 2 * bal * len(origins))
@@ -217,7 +245,7 @@
             h = hid[j, rows, :]
             for i in range(0, knz, 4):
                 w = jnp.concatenate([down[j * knz + i + e] for e in range(4)], axis=1)
-                p = jnp.dot(h, w, preferred_element_type=f32).astype(bf16)
+                p = jnp.dot(h, w, preferred_element_type=f32)
                 for e in range(4):
                     prod[j * knz + i + e, rows, :] = p[:, e * bd:(e + 1) * bd]
         loop(nj, down_row)
@@ -226,9 +254,9 @@
             def some(i):
                 for e in range(2):
                     b = q * (nblk // CHUNKS) + 2 * i + e
-                    acc = prod[inv[0, b], rows, :].astype(f32)
+                    acc = prod[inv[0, b], rows, :]
                     for j in range(1, nj):
-                        acc += prod[inv[j, b], rows, :].astype(f32)
+                        acc += prod[inv[j, b], rows, :]
                     cols = pl.ds(pl.multiple_of(b * bd, bd), bd)
                     acc = acc.astype(bf16)
                     for r, o in enumerate(origins):
@@ -238,52 +266,24 @@
             loop(nblk // CHUNKS // 2, some)
             for o in origins:
                 part_copy(o, q).start()
+            if last is not None:
+                @pl.when(last & (q > 0))
+                def _():
+                    hop(tau, q - 1)
         loop(CHUNKS, gather)
-
-    def hop(tau, q):
-        cols = cols_of(q)
-
-        def pass_on(t, has_more, slot_in, mp):
-            part_copy(t, q).wait_recv()
-            acc = part[t, :, cols].astype(f32) + sibin[t, :, cols].astype(f32)
-
-            @pl.when(has_more)
-            def _():
-                rs_copy(t, q, twin, slot_in).wait_recv()
-                part[t, :, cols] = (acc + rsin[slot_in, :, cols].astype(f32)).astype(bf16)
-
-            @pl.when(jnp.logical_not(has_more))
-            def _():
-                part[t, :, cols] = acc.astype(bf16)
-            rs_copy(t, q, mp, slot_in).start()
-
-        left = 2 * (n - 1) - z - tau
-
-        @pl.when((left >= 0) & (left < z))
-        def _():
-            pass_on(left, z < n - 1, left, m - 2)
-        right = tau - z
-
-        @pl.when((right > z) & (right < n))
-        def _():
-            pass_on(right, z > 0, n + right, m + 2)
-
-    def near(i):
-        o = z + 2 * i - 1
-
-        @pl.when(at_end & (o >= 0) & (o < n))
-        def _():
-            unit([z, o], 1, None)
-    loop(2, near)
-    if n > 2:
-        @pl.when(jnp.logical_not(at_end))
-        def _():
-            unit([z, z - 1, z + 1], 1, z >= 0)
-    loop(CHUNKS, lambda q: hop(1, q))
+        if last is not None:
+            @pl.when(last)
+            def _():
+                hop(tau, CHUNKS - 1)
+
+    unit([z], 0, None)
 
     def phase(i):
-        tau = i + 2
-        loop(CHUNKS, lambda q: take_all(tau, q, False))
+        tau = i + 1
+
+        @pl.when(tau > 1)
+        def _():
+            loop(CHUNKS, lambda q: take_all(tau, q, False))
 
         def side(i):
             o = z + (2 * i - 1) * tau
@@ -292,8 +292,11 @@
             def _():
                 unit([o], tau, (i == 1) | (z + tau >= n))
         loop(2, side)
-        loop(CHUNKS, lambda q: hop(tau, q))
-    loop(n - 2, phase)
+
+        @pl.when((z - tau < 0) & (z + tau >= n))
+        def _():
+            loop(CHUNKS, lambda q: hop(tau, q))
+    loop(n - 1, phase)
 
     def finish(q):
         cols = cols_of(q)
@@ -363,7 +366,7 @@
     vm, sm, hbm = (pl.BlockSpec(memory_space=s) for s in (pltpu.VMEM, pltpu.SMEM, pl.ANY))
     dma = pltpu.SemaphoreType.DMA
     rows = n * 2 * bal
-    tall = 2 * bal * min(n, 3)
+    tall = 2 * bal
     return pl.pallas_call(
         functools.partial(kernel, ndp, n, sl),
         out_shape=jax.ShapeDtypeStruct(tokens.shape, bf16),
@@ -379,7 +382,7 @@
             pltpu.VMEM((n, bal, width), bf16),
             pltpu.VMEM((nblk, tall, bd), bf16),
             pltpu.VMEM((nj, tall, bf), bf16),
-            pltpu.VMEM((nj * knz + 1, tall, bd), bf16),
+            pltpu.VMEM((nj * knz + 1, tall, bd), jnp.float32),
             pltpu.VMEM((bal, width // CHUNKS), jnp.float32),
             pltpu.VMEM((n, bal, width), bf16),
             pltpu.VMEM((n, bal, width), bf16),

time: 102 us -> 124 us (1.22)
  Pallas kernels: 98.1 us -> 120 us
    pallas_call x1, Pallas kernels: 98.1 us -> 120 us  [body(): pl.pallas_call(functools.partial(kernel, ndp, n, sl), out_shape=jax.Shape...]
where the time goes in v4:
time: 124 us
  Pallas kernels  120 us (97%)
  local copies, waits for them, and re-layouts  2.26 us (2%)
  other arithmetic  1.4 us (1%)
    pallas_call x1, Pallas kernels, body(): pl.pallas_call(functools.partial(kernel, ndp, n, sl), out_shape=jax.Shape...  120 us

profile of v4, /device:TPU:0, one launch (start us, length us, event | category | flops | bytes accessed | tf_op | source)
XLA Modules:
  0.0 123.9 jit_solution(5969404439081166951)
XLA Ops:
  0.0 1.4 %select_reduce_fusion.inv = s32[8,64]{1,0:T(8,128)} fusion(s32[8,16]{1,0:T(8,128)S(1)} %multiply_add_fusion, s32[8,16]{1,0:T(8,128)} %param.15), kind=kLoop, calls=%fused_computation | loop fusion | flops 24064 | bytes 3072 | tf_op jit(solution)/shard_map/reduce_min | solution.py:364
  1.4 120.2 %shard_map.82 = bf16[64,8192]{1,0:T(8,128)(2,1)} custom-call(bf16[64,8192]{1,0:T(8,128)(2,1)} %tok.1, s32[4,8]{1,0:T(4,128)} %cnt.1, bf16[8,2048,256]{2,1,0:T(8,128)(2,1)} %bitcast.3, s32[8,16]{1,0:T(8,128)} %gi.1, bf16[8,2048,256]{2,1,0:T(8,128)(2,1)} %bitcast.4, s32[8,16]{1,0:T(8,128)} %ui.1, bf16[128,256,128]{2,1,0:T(8,128)(2,1)} %bitcast.5, ...), custom_call_target="tpu_custom_call" | custom-call | flops 6442450944 | bytes 25165824 | tf_op jit(solution)/shard_map/pallas_call | solution.py:370
  121.6 2.3 %copy.10 = bf16[64,8192]{1,0:T(8,128)(2,1)} copy(bf16[64,8192]{1,0:T(8,128)(2,1)} %shard_map.82) | data formatting | bytes 2097152
  (1 shorter events, 0.0 us)

commit v5 on v4

--- a/solution.py
+++ b/solution.py
@@ -8,7 +8,7 @@
 from jax.sharding import PartitionSpec as P
 
 MESH = pl.DeviceIdType.MESH
-CHUNKS = 8
+CHUNKS = 4
 
 
 def kernel(
@@ -170,14 +170,7 @@
         def _():
             ag_copy(z, q, m - 2, n).start()
         twin_copy(z, q).start()
-
-        @pl.when(q > 0)
-        def _():
-            take_all(1, q - 1, True)
-            take_all(1, q - 1, False)
     loop(CHUNKS, spread)
-    take_all(1, CHUNKS - 1, True)
-    take_all(1, CHUNKS - 1, False)
     for load in loads:
         load.wait()
 
@@ -234,19 +227,19 @@
                 gv = jnp.dot(picked(gi), gate[j], preferred_element_type=f32)
                 uv = jnp.dot(picked(ui), up[j], preferred_element_type=f32)
                 hid[j, rows, :] = (gv / (1.0 + jnp.exp(-gv)) * uv).astype(bf16)
-            if last is not None:
-                @pl.when(last)
-                def _():
-                    for i in range(passes):
-                        take_all(tau + 1, g * passes + i, True)
+
+            @pl.when(last)
+            def _():
+                for i in range(passes):
+                    take_all(tau + 1, g * passes + i, True)
         loop(steps, columns)
 
         def down_row(j):
             h = hid[j, rows, :]
-            for i in range(0, knz, 4):
-                w = jnp.concatenate([down[j * knz + i + e] for e in range(4)], axis=1)
+            for i in range(0, knz, 2):
+                w = jnp.concatenate([down[j * knz + i + e] for e in range(2)], axis=1)
                 p = jnp.dot(h, w, preferred_element_type=f32)
-                for e in range(4):
+                for e in range(2):
                     prod[j * knz + i + e, rows, :] = p[:, e * bd:(e + 1) * bd]
         loop(nj, down_row)
 
@@ -266,24 +259,13 @@
             loop(nblk // CHUNKS // 2, some)
             for o in origins:
                 part_copy(o, q).start()
-            if last is not None:
-                @pl.when(last & (q > 0))
-                def _():
-                    hop(tau, q - 1)
         loop(CHUNKS, gather)
-        if last is not None:
-            @pl.when(last)
-            def _():
-                hop(tau, CHUNKS - 1)
-
-    unit([z], 0, None)
+
+    unit([z], 0, z >= 0)
 
     def phase(i):
         tau = i + 1
-
-        @pl.when(tau > 1)
-        def _():
-            loop(CHUNKS, lambda q: take_all(tau, q, False))
+        loop(CHUNKS, lambda q: take_all(tau, q, False))
 
         def side(i):
             o = z + (2 * i - 1) * tau
@@ -292,17 +274,13 @@
             def _():
                 unit([o], tau, (i == 1) | (z + tau >= n))
         loop(2, side)
-
-        @pl.when((z - tau < 0) & (z + tau >= n))
-        def _():
-            loop(CHUNKS, lambda q: hop(tau, q))
+        loop(CHUNKS, lambda q: hop(tau, q))
     loop(n - 1, phase)
 
     def finish(q):
         cols = cols_of(q)
         for s in range(1, ndp):
             exchange(sendp, recvp, x_s, x_r, s, q).wait_send()
-        loop(n - 1, lambda i: hop(n + i, q))
         part_copy(z, q).wait_recv()
         total[...] = part[z, :, cols].astype(f32) + sibin[z, :, cols].astype(f32)
 
@@ -319,7 +297,20 @@
         for s in range(1, ndp):
             exchange(sendp, back, bk_s, bk_r, s, q).start()
         back[slab(d), cols] = sendp[slab(d), cols]
-    loop(CHUNKS, finish)
+
+    def tail(turn):
+        for i in range(n - 1):
+            q = turn - i
+
+            @pl.when((q >= 0) & (q < CHUNKS))
+            def _():
+                hop(n + i, q)
+        q = turn - (n - 1)
+
+        @pl.when(q >= 0)
+        def _():
+            finish(q)
+    loop(CHUNKS + n - 1, tail)
 
     def store(q):
         cols = cols_of(q)

time: 124 us -> 93.9 us (0.76)
  Pallas kernels: 120 us -> 90 us
    pallas_call x1, Pallas kernels: 120 us -> 90 us  [body(): pl.pallas_call(functools.partial(kernel, ndp, n, sl), out_shape=jax.Shape...]
where the time goes in v5:
time: 93.9 us; the launch traced here: 93.7 us
  Pallas kernels  90 us (96%)
  local copies, waits for them, and re-layouts  2.26 us (2%)
  other arithmetic  1.4 us (1%)
    pallas_call x1, Pallas kernels, body(): pl.pallas_call(functools.partial(kernel, ndp, n, sl), out_shape=jax.Shape...  90 us
    unnamed x1, local copies, waits for them, and re-layouts  2.26 us

profile of v5, /device:TPU:0, one launch (start us, length us, event | category | flops | bytes accessed | tf_op | source)
XLA Modules:
  0.0 93.7 jit_solution(10684955828554557624)
XLA Ops:
  0.0 1.4 %select_reduce_fusion.inv = s32[8,64]{1,0:T(8,128)} fusion(s32[8,16]{1,0:T(8,128)S(1)} %multiply_add_fusion, s32[8,16]{1,0:T(8,128)} %param.15), kind=kLoop, calls=%fused_computation | loop fusion | flops 24064 | bytes 3072 | tf_op jit(solution)/shard_map/reduce_min | solution.py:355
  1.4 90.0 %shard_map.82 = bf16[64,8192]{1,0:T(8,128)(2,1)} custom-call(bf16[64,8192]{1,0:T(8,128)(2,1)} %tok.1, s32[4,8]{1,0:T(4,128)} %cnt.1, bf16[8,2048,256]{2,1,0:T(8,128)(2,1)} %bitcast.3, s32[8,16]{1,0:T(8,128)} %gi.1, bf16[8,2048,256]{2,1,0:T(8,128)(2,1)} %bitcast.4, s32[8,16]{1,0:T(8,128)} %ui.1, bf16[128,256,128]{2,1,0:T(8,128)(2,1)} %bitcast.5, ...), custom_call_target="tpu_custom_call" | custom-call | flops 6442450944 | bytes 25165824 | tf_op jit(solution)/shard_map/pallas_call | solution.py:361
  91.4 2.3 %copy.10 = bf16[64,8192]{1,0:T(8,128)(2,1)} copy(bf16[64,8192]{1,0:T(8,128)(2,1)} %shard_map.82) | data formatting | bytes 2097152
  (1 shorter events, 0.0 us)

commit v6 on v5

--- a/solution.py
+++ b/solution.py
@@ -8,7 +8,8 @@
 from jax.sharding import PartitionSpec as P
 
 MESH = pl.DeviceIdType.MESH
-CHUNKS = 4
+CHUNKS = 8
+SKEW = 2
 
 
 def kernel(
@@ -202,7 +203,7 @@
         def _():
             pass_on(right, z > 0, n + right, m + 2)
 
-    def unit(origins, tau, last):
+    def unit(origins, tau, passing):
         rows = pl.ds(0, 2 * bal * len(origins))
 
         def wait_rows(q):
@@ -228,7 +229,7 @@
                 uv = jnp.dot(picked(ui), up[j], preferred_element_type=f32)
                 hid[j, rows, :] = (gv / (1.0 + jnp.exp(-gv)) * uv).astype(bf16)
 
-            @pl.when(last)
+            @pl.when(passing)
             def _():
                 for i in range(passes):
                     take_all(tau + 1, g * passes + i, True)
@@ -272,7 +273,7 @@
 
             @pl.when((o >= 0) & (o < n))
             def _():
-                unit([o], tau, (i == 1) | (z + tau >= n))
+                unit([o], tau, (i == 0) | (z - tau < 0))
         loop(2, side)
         loop(CHUNKS, lambda q: hop(tau, q))
     loop(n - 1, phase)
@@ -299,18 +300,18 @@
         back[slab(d), cols] = sendp[slab(d), cols]
 
     def tail(turn):
-        for i in range(n - 1):
-            q = turn - i
+        for i in range(n - 2):
+            q = turn - i * SKEW
 
             @pl.when((q >= 0) & (q < CHUNKS))
             def _():
                 hop(n + i, q)
-        q = turn - (n - 1)
+        q = turn - (n - 2) * SKEW
 
         @pl.when(q >= 0)
         def _():
             finish(q)
-    loop(CHUNKS + n - 1, tail)
+    loop(CHUNKS + (n - 2) * SKEW, tail)
 
     def store(q):
         cols = cols_of(q)

time: 93.9 us -> 95.2 us (1.014)
  Pallas kernels: 90 us -> 91.3 us
    pallas_call x1, Pallas kernels: 90 us -> 91.3 us  [body(): pl.pallas_call(functools.partial(kernel, ndp, n, sl), out_shape=jax.Shape...]
where the time goes in v6:
time: 95.2 us; the launch traced here: 95 us
  Pallas kernels  91.3 us (96%)
  local copies, waits for them, and re-layouts  2.26 us (2%)
  other arithmetic  1.4 us (1%)
    pallas_call x1, Pallas kernels, body(): pl.pallas_call(functools.partial(kernel, ndp, n, sl), out_shape=jax.Shape...  91.3 us
    unnamed x1, local copies, waits for them, and re-layouts  2.26 us

profile of v6, /device:TPU:0, one launch (start us, length us, event | category | flops | bytes accessed | tf_op | source)
XLA Modules:
  0.0 95.0 jit_solution(6791701406012641617)
XLA Ops:
  0.0 1.4 %select_reduce_fusion.inv = s32[8,64]{1,0:T(8,128)} fusion(s32[8,16]{1,0:T(8,128)S(1)} %multiply_add_fusion, s32[8,16]{1,0:T(8,128)} %param.15), kind=kLoop, calls=%fused_computation | loop fusion | flops 24064 | bytes 3072 | tf_op jit(solution)/shard_map/reduce_min | solution.py:356
  1.4 91.3 %shard_map.82 = bf16[64,8192]{1,0:T(8,128)(2,1)} custom-call(bf16[64,8192]{1,0:T(8,128)(2,1)} %tok.1, s32[4,8]{1,0:T(4,128)} %cnt.1, bf16[8,2048,256]{2,1,0:T(8,128)(2,1)} %bitcast.3, s32[8,16]{1,0:T(8,128)} %gi.1, bf16[8,2048,256]{2,1,0:T(8,128)(2,1)} %bitcast.4, s32[8,16]{1,0:T(8,128)} %ui.1, bf16[128,256,128]{2,1,0:T(8,128)(2,1)} %bitcast.5, ...), custom_call_target="tpu_custom_call" | custom-call | flops 6442450944 | bytes 25165824 | tf_op jit(solution)/shard_map/pallas_call | solution.py:362
  92.7 2.3 %copy.10 = bf16[64,8192]{1,0:T(8,128)(2,1)} copy(bf16[64,8192]{1,0:T(8,128)(2,1)} %shard_map.82) | data formatting | bytes 2097152
  (1 shorter events, 0.0 us)

commit v7 on v6

--- a/solution.py
+++ b/solution.py
@@ -8,8 +8,8 @@
 from jax.sharding import PartitionSpec as P
 
 MESH = pl.DeviceIdType.MESH
-CHUNKS = 8
-SKEW = 2
+CHUNKS = 4
+SKEW = 1
 
 
 def kernel(
@@ -237,17 +237,17 @@
 
         def down_row(j):
             h = hid[j, rows, :]
-            for i in range(0, knz, 2):
-                w = jnp.concatenate([down[j * knz + i + e] for e in range(2)], axis=1)
+            for i in range(0, knz, 4):
+                w = jnp.concatenate([down[j * knz + i + e] for e in range(4)], axis=1)
                 p = jnp.dot(h, w, preferred_element_type=f32)
-                for e in range(2):
+                for e in range(4):
                     prod[j * knz + i + e, rows, :] = p[:, e * bd:(e + 1) * bd]
         loop(nj, down_row)
 
         def gather(q):
             def some(i):
-                for e in range(2):
-                    b = q * (nblk // CHUNKS) + 2 * i + e
+                for e in range(4):
+                    b = q * (nblk // CHUNKS) + 4 * i + e
                     acc = prod[inv[0, b], rows, :]
                     for j in range(1, nj):
                         acc += prod[inv[j, b], rows, :]
@@ -257,7 +257,7 @@
                         top = 2 * bal * r
                         part[o, :, cols] = acc[top:top + bal]
                         sibout[o, :, cols] = acc[top + bal:top + 2 * bal]
-            loop(nblk // CHUNKS // 2, some)
+            loop(nblk // CHUNKS // 4, some)
             for o in origins:
                 part_copy(o, q).start()
         loop(CHUNKS, gather)

time: 95.2 us -> 94 us (0.987)
  Pallas kernels: 91.3 us -> 90.1 us
    pallas_call x1, Pallas kernels: 91.3 us -> 90.1 us  [body(): pl.pallas_call(functools.partial(kernel, ndp, n, sl), out_shape=jax.Shape...]
where the time goes in v7:
time: 94 us; the launch traced here: 93.8 us
  Pallas kernels  90.1 us (96%)
  local copies, waits for them, and re-layouts  2.26 us (2%)
  other arithmetic  1.4 us (1%)
    pallas_call x1, Pallas kernels, body(): pl.pallas_call(functools.partial(kernel, ndp, n, sl), out_shape=jax.Shape...  90.1 us
    unnamed x1, local copies, waits for them, and re-layouts  2.26 us

profile of v7, /device:TPU:0, one launch (start us, length us, event | category | flops | bytes accessed | tf_op | source)
XLA Modules:
  0.0 93.8 jit_solution(13085983894659962353)
XLA Ops:
  0.0 1.4 %select_reduce_fusion.inv = s32[8,64]{1,0:T(8,128)} fusion(s32[8,16]{1,0:T(8,128)S(1)} %multiply_add_fusion, s32[8,16]{1,0:T(8,128)} %param.15), kind=kLoop, calls=%fused_computation | loop fusion | flops 24064 | bytes 3072 | tf_op jit(solution)/shard_map/reduce_min | solution.py:356
  1.4 90.1 %shard_map.82 = bf16[64,8192]{1,0:T(8,128)(2,1)} custom-call(bf16[64,8192]{1,0:T(8,128)(2,1)} %tok.1, s32[4,8]{1,0:T(4,128)} %cnt.1, bf16[8,2048,256]{2,1,0:T(8,128)(2,1)} %bitcast.3, s32[8,16]{1,0:T(8,128)} %gi.1, bf16[8,2048,256]{2,1,0:T(8,128)(2,1)} %bitcast.4, s32[8,16]{1,0:T(8,128)} %ui.1, bf16[128,256,128]{2,1,0:T(8,128)(2,1)} %bitcast.5, ...), custom_call_target="tpu_custom_call" | custom-call | flops 6442450944 | bytes 25165824 | tf_op jit(solution)/shard_map/pallas_call | solution.py:362
  91.5 2.3 %copy.10 = bf16[64,8192]{1,0:T(8,128)(2,1)} copy(bf16[64,8192]{1,0:T(8,128)(2,1)} %shard_map.82) | data formatting | bytes 2097152
  (1 shorter events, 0.0 us)

commit v8 on v5

--- a/solution.py
+++ b/solution.py
@@ -299,18 +299,18 @@
         back[slab(d), cols] = sendp[slab(d), cols]
 
     def tail(turn):
-        for i in range(n - 1):
+        for i in range(n - 2):
             q = turn - i
 
             @pl.when((q >= 0) & (q < CHUNKS))
             def _():
                 hop(n + i, q)
-        q = turn - (n - 1)
+        q = turn - (n - 2)
 
         @pl.when(q >= 0)
         def _():
             finish(q)
-    loop(CHUNKS + n - 1, tail)
+    loop(CHUNKS + n - 2, tail)
 
     def store(q):
         cols = cols_of(q)

time: 93.9 us -> 93.9 us (level)
  no operation moved by 1% of the time
where the time goes in v8:
time: 93.9 us; the launch traced here: 93.7 us
  Pallas kernels  90 us (96%)
  local copies, waits for them, and re-layouts  2.26 us (2%)
  other arithmetic  1.4 us (1%)
    pallas_call x1, Pallas kernels, body(): pl.pallas_call(functools.partial(kernel, ndp, n, sl), out_shape=jax.Shape...  90 us
    unnamed x1, local copies, waits for them, and re-layouts  2.26 us

profile of v8, /device:TPU:0, one launch (start us, length us, event | category | flops | bytes accessed | tf_op | source)
XLA Modules:
  0.0 93.7 jit_solution(16454068471248216455)
XLA Ops:
  0.0 1.4 %select_reduce_fusion.inv = s32[8,64]{1,0:T(8,128)} fusion(s32[8,16]{1,0:T(8,128)S(1)} %multiply_add_fusion, s32[8,16]{1,0:T(8,128)} %param.15), kind=kLoop, calls=%fused_computation | loop fusion | flops 24064 | bytes 3072 | tf_op jit(solution)/shard_map/reduce_min | solution.py:355
  1.4 90.0 %shard_map.82 = bf16[64,8192]{1,0:T(8,128)(2,1)} custom-call(bf16[64,8192]{1,0:T(8,128)(2,1)} %tok.1, s32[4,8]{1,0:T(4,128)} %cnt.1, bf16[8,2048,256]{2,1,0:T(8,128)(2,1)} %bitcast.3, s32[8,16]{1,0:T(8,128)} %gi.1, bf16[8,2048,256]{2,1,0:T(8,128)(2,1)} %bitcast.4, s32[8,16]{1,0:T(8,128)} %ui.1, bf16[128,256,128]{2,1,0:T(8,128)(2,1)} %bitcast.5, ...), custom_call_target="tpu_custom_call" | custom-call | flops 6442450944 | bytes 25165824 | tf_op jit(solution)/shard_map/pallas_call | solution.py:361
  91.4 2.3 %copy.10 = bf16[64,8192]{1,0:T(8,128)(2,1)} copy(bf16[64,8192]{1,0:T(8,128)(2,1)} %shard_map.82) | data formatting | bytes 2097152
  (1 shorter events, 0.0 us)
